TPU v7x, 512 devices: a whole 4x4x16 slice. The times are simulated.
512 devices in a mesh: gx: 16 (over z), gy: 8 (over x_lo, y), gz: 4 (over x_hi, core).
Axes of the slice: x: 4 (x_hi: 2, x_lo: 2; x = x_hi * 2 + x_lo), y: 4, z: 16, core: 2. Of those that a mesh axis runs over, the one named last changes fastest.
Arguments:
- atom_x: float32 [16, 32, 256], P('gx', ('gy', 'gz')), may hold values from 0 to 23.99
- atom_y: float32 [16, 32, 256], P('gx', ('gy', 'gz')), may hold values from 0 to 11.99
- atom_z: float32 [16, 32, 256], P('gx', ('gy', 'gz')), may hold values from 0 to 384
- charges: float32 [16, 32, 256], P('gx', ('gy', 'gz')), may hold values from -4.5 to 4.5
- counts: int32 [16, 32], P('gx', ('gy', 'gz')), may hold values from 32 to 256, as said below
- background: float32 [384, 384, 384], P(('gy', 'gz'), 'gx'), may hold values from -0.3125 to 0.3125
Outputs:
- forces: float32 [3, 16, 32, 256], P(None, 'gx', ('gy', 'gz'))
Inputs may be any that keep to these rules, and one draw needn't show every extreme that they name: `counts`: live slots come first in each pencil; some pencil is full in every draw.
All inputs are finite; a program needn't handle non-finite values.
Results may differ from a plain program's by a relative error of at most 0.0003.
Values sent between devices are 32-bit elements; how exact they have to be, the bound alone decides.
A program may use at most 128 MiB of HBM per device.

v0:
```python
import math

import jax
import jax.numpy as jnp
import ml_dtypes
import numpy as np
from jax import lax
from jax.experimental import pallas as pl
from jax.experimental.pallas import tpu as pltpu
from jax.sharding import PartitionSpec as P

COULOMB = 6.5
N = 384
RING = 16
ROWS = 32
CX, CY = N // RING, N // ROWS
EX, EY = 32, 16
KX = 28
SLOTS = 256
CHUNKS = 3
UNITS = 36
MESH = pl.DeviceIdType.MESH
F32 = jnp.float32
BF16 = jnp.bfloat16


def parts(table):
    high = table.astype(ml_dtypes.bfloat16)
    low = (table - high.astype(np.float64)).astype(ml_dtypes.bfloat16)
    return high, low


def cas(rows, columns):
    angles = (rows[:, None] * columns[None, :] % N) * (2.0 * math.pi / N)
    return np.cos(angles) + np.sin(angles)


def wide_table(table):
    high, low = parts(table)
    return np.concatenate([high, low, high], axis=1)


def tall_table(table):
    high, low = parts(table)
    return np.concatenate([high, low, high], axis=0)


def make_tables():
    wave = np.arange(N)
    along_z = wide_table(cas(wave, wave))
    inner_y = np.arange(EY)
    inner_y = np.where(inner_y < CY + 2, inner_y, inner_y - EY)
    cell_y = (inner_y[:, None] + CY * np.arange(ROWS)[None, :]).reshape(-1) % N
    ahead_y = tall_table(cas(cell_y, wave))
    back_y = tall_table(cas(wave, cell_y))
    inner_x = np.arange(EX)
    used = np.tile(inner_x < KX, RING)
    inner_x = np.where(inner_x < CX + 2, inner_x, inner_x - KX)
    cell_x = (CX * np.arange(RING)[:, None] + inner_x[None, :]).reshape(-1) % N
    matrix_x = cas(wave, cell_x) * used[None, :]
    ahead_x = wide_table(matrix_x)
    back_x = wide_table(matrix_x.T)
    signed = np.where(wave <= N // 2, wave, wave - N) / N
    angles = 2.0 * math.pi / N * wave
    modulus = (230.0 + 152.0 * np.cos(angles) + 2.0 * np.cos(2.0 * angles)) / 384.0
    decay = np.exp(-(math.pi**2) * signed**2) / modulus**2
    factor = COULOMB / (math.pi * N * N * N)
    green_x = np.broadcast_to(np.stack([decay, signed**2])[:, :, None], (2, N, 128))
    green_y = np.stack([decay * factor, signed**2]).reshape(2, 3, 1, 128)
    green_y = np.broadcast_to(green_y, (2, 3, 8, 128))
    return (
        along_z,
        ahead_y,
        back_y,
        ahead_x,
        back_x,
        np.ascontiguousarray(green_x, dtype=np.float32),
        np.ascontiguousarray(green_y, dtype=np.float32),
    )


def spline(offset):
    distance = jnp.minimum(offset, 5.0 - offset)
    ramp_zero = jnp.maximum(distance, 0.0)
    ramp_one = jnp.maximum(distance - 1.0, 0.0)
    ramp_two = jnp.maximum(distance - 2.0, 0.0)
    cube_zero = ramp_zero * ramp_zero * ramp_zero
    cube_one = ramp_one * ramp_one * ramp_one
    cube_two = ramp_two * ramp_two * ramp_two
    height = (cube_zero * ramp_zero - 5.0 * cube_one * ramp_one + 10.0 * cube_two * ramp_two) * (
        1.0 / 24.0
    )
    gradient = (cube_zero - 5.0 * cube_one + 10.0 * cube_two) * (1.0 / 6.0)
    return height, jnp.where(offset < 2.5, gradient, -gradient)


def halves(value):
    high = value.astype(BF16)
    return high, (value - high.astype(F32)).astype(BF16)


def dot(left, right):
    return jnp.dot(left, right, preferred_element_type=F32)


def dot_nt(left, right):
    return lax.dot_general(left, right, (((1,), (1,)), ((), ())), preferred_element_type=F32)


def exchange_blocks(items):
    lane = lax.broadcasted_iota(jnp.int32, (8, 128), 1)
    low = lane < 64
    even = (lane // 32) % 2 == 0

    def pair(first, second, shift, mask):
        back = pltpu.roll(second, shift, 1)
        ahead = pltpu.roll(first, 128 - shift, 1)
        return jnp.where(mask, first, back), jnp.where(mask, ahead, second)

    zero, two = pair(items[0], items[2], 64, low)
    one, three = pair(items[1], items[3], 64, low)
    zero, one = pair(zero, one, 32, even)
    two, three = pair(two, three, 32, even)
    return zero, one, two, three


def kernel(
    atom_x,
    atom_y,
    atom_z,
    charges,
    counts,
    background,
    table_z_hbm,
    ahead_y_hbm,
    back_y_hbm,
    ahead_x_hbm,
    back_x_hbm,
    green_x_hbm,
    green_y_hbm,
    out,
    table_z,
    ahead_y,
    back_y,
    ahead_x,
    back_x,
    green_x,
    green_y,
    table_sem,
    weight_z,
    slope_z,
    mixed,
    mixed_parts,
    charge,
    charge_parts,
    deposit_parts,
    pull_parts,
    lines,
    turned,
    spread_out,
    spread_in,
    wave_out,
    wave_in,
    back_out,
    back_in,
    cell_out,
    cell_in,
    gathered,
    send_one,
    recv_one,
    send_two,
    recv_two,
    send_three,
    recv_three,
    send_four,
    recv_four,
):
    ring = lax.axis_index("gx")
    major, minor = lax.axis_index("gy"), lax.axis_index("gz")
    row = major * 4 + minor
    core = lax.rem(minor, 2)

    def in_ring(index):
        return (index, major, minor)

    def in_rows(index):
        return (ring, lax.div(index, 4), lax.rem(index, 4))

    barrier = pltpu.get_barrier_semaphore()

    @pl.loop(1, ROWS)
    def _(step):
        pl.semaphore_signal(
            barrier, inc=1, device_id=in_rows(lax.rem(row + step, ROWS)), device_id_type=MESH
        )

    @pl.loop(1, RING)
    def _(step):
        pl.semaphore_signal(
            barrier, inc=1, device_id=in_ring(lax.rem(ring + step, RING)), device_id_type=MESH
        )

    tables = [
        pltpu.make_async_copy(source, target, table_sem.at[place])
        for place, (source, target) in enumerate(
            (
                (table_z_hbm, table_z),
                (ahead_y_hbm, ahead_y),
                (ahead_x_hbm, ahead_x),
                (green_x_hbm, green_x),
                (green_y_hbm, green_y),
                (back_x_hbm, back_x),
                (back_y_hbm, back_y),
            )
        )
    ]
    for copy in tables:
        copy.start()

    wave_in[:, :, KX:, :] = jnp.zeros((3, RING, EX - KX, 128), F32)
    back_in[:, KX:, :] = jnp.zeros((UNITS, EX - KX, 128), F32)

    slot = lax.broadcasted_iota(jnp.int32, (1, SLOTS), 1)
    live = jnp.where(slot < counts[0, 0], charges[0], 0.0)
    inner_y = lax.broadcasted_iota(jnp.int32, (EY, SLOTS), 0)
    inner_y = jnp.where(inner_y < CY + 2, inner_y, inner_y - EY).astype(F32)
    height_y, slope_y = spline(atom_y[0] - inner_y + 2.5)
    inner_x = lax.broadcasted_iota(jnp.int32, (EX, SLOTS), 0)
    used = inner_x < KX
    inner_x = jnp.where(inner_x < CX + 2, inner_x, inner_x - KX).astype(F32)
    height_x, slope_x = spline(atom_x[0] - inner_x + 2.5)
    height_x = jnp.where(used, height_x, 0.0)
    slope_x = jnp.where(used, slope_x, 0.0)

    @pl.loop(0, N // 64)
    def _(block):
        first = pl.multiple_of(block * 64, 64)
        plane = (lax.broadcasted_iota(jnp.int32, (64, SLOTS), 0) + first).astype(F32)
        offset = atom_z[0] - plane
        offset = jnp.where(offset >= N / 2.0, offset - N, offset)
        offset = jnp.where(offset < -N / 2.0, offset + N, offset)
        height, slope = spline(offset + 2.5)
        for value, target in ((height, weight_z), (slope, slope_z)):
            high, low = halves(value)
            target[pl.ds(first, 64), :] = high
            target[pl.ds(N + first, 64), :] = high
            target[pl.ds(2 * N + first, 64), :] = low

    charged_y = height_y * live
    for y in range(EY):
        for group in range(4):
            mixed[group * 128 + y * 8 : group * 128 + y * 8 + 8, :] = (
                height_x[group * 8 : group * 8 + 8] * charged_y[y : y + 1]
            )
    high, low = halves(mixed[...])
    mixed_parts[:, :SLOTS] = high
    mixed_parts[:, SLOTS : 2 * SLOTS] = high
    mixed_parts[:, 2 * SLOTS :] = low

    for group in range(3):
        for y in range(CY):
            charge[group * 128 + y * 8 : group * 128 + y * 8 + 8, :] = background[
                y, group * 8 : group * 8 + 8, :
            ]
        charge[group * 128 + CY * 8 : group * 128 + 128, :] = jnp.zeros((128 - CY * 8, N), F32)
    high, low = halves(charge[...])
    charge_parts[:, :N] = high
    charge_parts[:, N : 2 * N] = high
    charge_parts[:, 2 * N :] = low

    tables[0].wait()
    high, low = halves(dot(table_z[...], weight_z[...]))
    deposit_parts[:, :SLOTS] = high
    deposit_parts[:, SLOTS : 2 * SLOTS] = low
    deposit_parts[:, 2 * SLOTS :] = high
    for chunk in range(CHUNKS):
        for place, value in enumerate((high, low, high)):
            pull_parts[chunk, place * 128 : place * 128 + 128, :SLOTS] = value[
                chunk * 128 : chunk * 128 + 128
            ]

    pl.semaphore_wait(barrier, ROWS - 1 + RING - 1)

    spread_tiles = spread_out.reshape(CHUNKS, 4, 128, 128)

    @pl.loop(0, CHUNKS)
    def _(chunk):
        first = pl.multiple_of(chunk * 128, 128)
        atoms = dot_nt(deposit_parts[pl.ds(first, 128), :], mixed_parts[...])
        frozen = dot_nt(table_z[pl.ds(first, 128), :], charge_parts[...])
        for group in range(4):
            tile = atoms[:, group * 128 : group * 128 + 128]
            if group < 3:
                tile = tile + frozen[:, group * 128 : group * 128 + 128]
            spread_tiles[chunk, group] = tile
        pltpu.make_async_copy(
            spread_out.at[chunk, :, row], spread_in.at[chunk, :, :, row], recv_one.at[chunk]
        ).start()

        @pl.loop(1, ROWS)
        def _(step):
            target = lax.rem(row + step, ROWS)
            pltpu.make_async_remote_copy(
                spread_out.at[chunk, :, target],
                spread_in.at[chunk, :, :, row],
                send_one.at[chunk],
                recv_one.at[chunk],
                device_id=in_rows(target),
                device_id_type=MESH,
            ).start()

    high, low = halves(dot(table_z[...], slope_z[...]))
    for chunk in range(CHUNKS):
        for place, value in enumerate((high, low, high)):
            pull_parts[chunk, place * 128 : place * 128 + 128, SLOTS:] = value[
                chunk * 128 : chunk * 128 + 128
            ]

    tables[1].wait()
    spread_got = spread_in.reshape(CHUNKS, 4, 128, 128)

    @pl.loop(0, CHUNKS)
    def _(chunk):
        pltpu.make_async_copy(spread_in.at[chunk], spread_in.at[chunk], recv_one.at[chunk]).wait()
        for group in range(4):
            flipped = spread_got[chunk, group].T
            for quarter in range(4):
                items = [flipped[(quarter * 4 + j) * 8 : (quarter * 4 + j) * 8 + 8] for j in range(4)]
                for k, item in enumerate(exchange_blocks(items)):
                    lines[
                        k * EX + group * 8 : k * EX + group * 8 + 8,
                        quarter * 128 : quarter * 128 + 128,
                    ] = item
        high, low = halves(lines[...])
        waves = dot(jnp.concatenate([high, high, low], axis=1), ahead_y[...])
        for k in range(4):
            for tile in range(3):
                wave_out[chunk * 12 + k * 3 + tile] = waves[
                    k * EX : k * EX + EX, tile * 128 : tile * 128 + 128
                ]

        @pl.loop(0, 12)
        def _(step):
            unit = chunk * 12 + lax.rem(step + lax.div(3 * ring, 4), 12)
            target = lax.rem(5 * unit + 8 * core, RING)
            place = lax.div(unit, RING)

            @pl.when(target != ring)
            def _():
                pltpu.make_async_remote_copy(
                    wave_out.at[unit, 0:KX],
                    wave_in.at[place, ring, 0:KX],
                    send_two.at[unit],
                    recv_two.at[place],
                    device_id=in_ring(target),
                    device_id_type=MESH,
                ).start()

            @pl.when(target == ring)
            def _():
                pltpu.make_async_copy(
                    wave_out.at[unit, 0:KX], wave_in.at[place, ring, 0:KX], recv_two.at[place]
                ).start()

    for copy in tables[2:6]:
        copy.wait()
    base = lax.rem(13 * (ring + RING - 8 * core), RING)
    n_places = lax.div(UNITS - 1 - base, RING) + 1

    @pl.loop(0, n_places)
    def _(place):
        unit = place * RING + base
        pltpu.make_async_copy(
            wave_in.at[place, :, 0:KX], wave_in.at[place, :, 0:KX], recv_two.at[place]
        ).wait()
        high, low = halves(wave_in[place].reshape(RING * EX, 128))
        waves = dot(ahead_x[...], jnp.concatenate([high, high, low], axis=0))
        within = lax.rem(unit, 12)
        wave_z = lax.div(unit, 12) * 128 + row * 4 + lax.div(within, 3)
        tile = lax.rem(within, 3)
        decay = green_x[0, pl.ds(wave_z, 1), :] * green_y[0, tile]
        square = green_x[1, pl.ds(wave_z, 1), :] + green_y[1, tile]
        squares = green_x[1].reshape(N // 8, 8, 128) + square[None]
        decays = green_x[0].reshape(N // 8, 8, 128) * decay[None]
        green = jnp.where(squares > 0.0, decays / jnp.where(squares > 0.0, squares, 1.0), 0.0)
        high, low = halves(waves * green.reshape(N, 128))
        cells = dot(back_x[...], jnp.concatenate([high, high, low], axis=0))
        back_out[place] = cells.reshape(RING, EX, 128)
        group = lax.div(unit, 12)
        pltpu.make_async_copy(
            back_out.at[place, ring, 0:KX], back_in.at[unit, 0:KX], recv_three.at[group]
        ).start()

        @pl.loop(1, RING)
        def _(step):
            target = lax.rem(ring + step, RING)
            pltpu.make_async_remote_copy(
                back_out.at[place, target, 0:KX],
                back_in.at[unit, 0:KX],
                send_three.at[place, target],
                recv_three.at[group],
                device_id=in_ring(target),
                device_id_type=MESH,
            ).start()

    tables[6].wait()
    cell_tiles = cell_out.reshape(CHUNKS, 4, 128, 128)

    @pl.loop(0, CHUNKS)
    def _(chunk):
        units = pl.ds(chunk * 12, 12)
        pltpu.make_async_copy(
            back_in.at[units, 0:KX], back_in.at[units, 0:KX], recv_three.at[chunk]
        ).wait()
        tiles = [
            jnp.concatenate([back_in[chunk * 12 + k * 3 + tile] for tile in range(3)], axis=1)
            for k in range(4)
        ]
        high, low = halves(jnp.concatenate(tiles, axis=0))
        lines[...] = dot(jnp.concatenate([high, high, low], axis=1), back_y[...])
        for group in range(4):
            for quarter in range(4):
                items = [
                    lines[
                        k * EX + group * 8 : k * EX + group * 8 + 8,
                        quarter * 128 : quarter * 128 + 128,
                    ]
                    for k in range(4)
                ]
                for j, item in enumerate(exchange_blocks(items)):
                    turned[(quarter * 4 + j) * 8 : (quarter * 4 + j) * 8 + 8, :] = item
            cell_tiles[chunk, group] = turned[...].T
        pltpu.make_async_copy(
            cell_out.at[chunk, :, :, row], cell_in.at[chunk, :, row], recv_four.at[chunk]
        ).start()

        @pl.loop(1, ROWS)
        def _(step):
            target = lax.rem(row + step, ROWS)
            pltpu.make_async_remote_copy(
                cell_out.at[chunk, :, :, target],
                cell_in.at[chunk, :, row],
                send_four.at[chunk],
                recv_four.at[chunk],
                device_id=in_rows(target),
                device_id_type=MESH,
            ).start()

    cell_got = cell_in.reshape(CHUNKS, 4, 128, 128)
    gathered[...] = jnp.zeros((4 * 128, 2 * SLOTS), F32)

    @pl.loop(0, CHUNKS)
    def _(chunk):
        pltpu.make_async_copy(cell_in.at[chunk], cell_in.at[chunk], recv_four.at[chunk]).wait()
        for group in range(4):
            high, low = halves(cell_got[chunk, group].T)
            gathered[group * 128 : group * 128 + 128, :] += dot(
                jnp.concatenate([high, high, low], axis=1), pull_parts[chunk]
            )

    force_x = jnp.zeros((8, SLOTS), F32)
    force_y = jnp.zeros((8, SLOTS), F32)
    force_z = jnp.zeros((8, SLOTS), F32)
    for y in range(EY):
        along_x = jnp.zeros((8, SLOTS), F32)
        turned_x = jnp.zeros((8, SLOTS), F32)
        depth_x = jnp.zeros((8, SLOTS), F32)
        for group in range(4):
            first = group * 128 + y * 8
            plain = gathered[first : first + 8, :SLOTS]
            deriv = gathered[first : first + 8, SLOTS:]
            weight = height_x[group * 8 : group * 8 + 8]
            along_x += weight * plain
            turned_x += slope_x[group * 8 : group * 8 + 8] * plain
            depth_x += weight * deriv
        force_x += height_y[y : y + 1] * turned_x
        force_y += slope_y[y : y + 1] * along_x
        force_z += height_y[y : y + 1] * depth_x
    for place, force in enumerate((force_x, force_y, force_z)):
        out[place, 0] = -live * jnp.sum(force, axis=0, keepdims=True)

    @pl.loop(0, CHUNKS)
    def _(chunk):
        sizes = spread_out.at[chunk, :, 0 : ROWS - 1]
        pltpu.make_async_copy(sizes, sizes, send_one.at[chunk]).wait()
        sizes = cell_in.at[chunk, :, 0 : ROWS - 1]
        pltpu.make_async_copy(sizes, sizes, send_four.at[chunk]).wait()

    @pl.loop(0, UNITS)
    def _(unit):
        @pl.when(lax.rem(5 * unit + 8 * core, RING) != ring)
        def _():
            sizes = wave_out.at[unit, 0:KX]
            pltpu.make_async_copy(sizes, sizes, send_two.at[unit]).wait()

    @pl.loop(0, n_places)
    def _(place):
        @pl.loop(1, RING)
        def _(step):
            target = lax.rem(ring + step, RING)
            sizes = back_out.at[place, target, 0:KX]
            pltpu.make_async_copy(sizes, sizes, send_three.at[place, target]).wait()


def solution(mesh):
    tables = make_tables()

    def per_device(*args):
        vmem = pl.BlockSpec(memory_space=pltpu.VMEM)
        anywhere = pl.BlockSpec(memory_space=pl.ANY)
        held = [pltpu.VMEM(tables[place].shape, tables[place].dtype) for place in range(7)]
        return pl.pallas_call(
            kernel,
            out_shape=jax.ShapeDtypeStruct((3, 1, 1, SLOTS), F32),
            in_specs=[vmem] * 4 + [pl.BlockSpec(memory_space=pltpu.SMEM), vmem] + [anywhere] * 7,
            out_specs=vmem,
            scratch_shapes=held
            + [
                pltpu.SemaphoreType.DMA((7,)),
                pltpu.VMEM((3 * N, SLOTS), BF16),
                pltpu.VMEM((3 * N, SLOTS), BF16),
                pltpu.VMEM((4 * 128, SLOTS), F32),
                pltpu.VMEM((4 * 128, 3 * SLOTS), BF16),
                pltpu.VMEM((3 * 128, N), F32),
                pltpu.VMEM((3 * 128, 3 * N), BF16),
                pltpu.VMEM((N, 3 * SLOTS), BF16),
                pltpu.VMEM((CHUNKS, 3 * 128, 2 * SLOTS), BF16),
                pltpu.VMEM((4 * EX, EY * ROWS), F32),
                pltpu.VMEM((128, 128), F32),
                pltpu.VMEM((CHUNKS, 4, ROWS, 4, 1, 128), F32),
                pltpu.VMEM((CHUNKS, 4, 4, ROWS, 1, 128), F32),
                pltpu.VMEM((UNITS, EX, 128), F32),
                pltpu.VMEM((3, RING, EX, 128), F32),
                pltpu.VMEM((3, RING, EX, 128), F32),
                pltpu.VMEM((UNITS, EX, 128), F32),
                pltpu.VMEM((CHUNKS, 4, 4, ROWS, 1, 128), F32),
                pltpu.VMEM((CHUNKS, 4, ROWS, 4, 1, 128), F32),
                pltpu.VMEM((4 * 128, 2 * SLOTS), F32),
                pltpu.SemaphoreType.DMA((CHUNKS,)),
                pltpu.SemaphoreType.DMA((CHUNKS,)),
                pltpu.SemaphoreType.DMA((UNITS,)),
                pltpu.SemaphoreType.DMA((3,)),
                pltpu.SemaphoreType.DMA((3, RING)),
                pltpu.SemaphoreType.DMA((CHUNKS,)),
                pltpu.SemaphoreType.DMA((CHUNKS,)),
                pltpu.SemaphoreType.DMA((CHUNKS,)),
            ],
            compiler_params=pltpu.CompilerParams(
                collective_id=0, has_side_effects=True, vmem_limit_bytes=40 * 1024 * 1024
            ),
            name="ewald",
        )(*args, *(jnp.asarray(table) for table in tables))

    pencils = P("gx", ("gy", "gz"), None)
    return jax.shard_map(
        per_device,
        mesh=mesh,
        in_specs=(pencils,) * 4 + (P("gx", ("gy", "gz")), P(("gy", "gz"), "gx", None)),
        out_specs=P(None, "gx", ("gy", "gz"), None),
        check_vma=False,
    )
```

profile of v0, /device:TPU:1, one launch (start us, length us, event | category | flops | bytes accessed | tf_op | source)
XLA Modules:
  0.0 96.9 jit_solution(6698415350506298660)
XLA Ops:
  0.7 0.0 copy-start
  0.7 1.3 %copy-done = bf16[512,1152]{1,0:T(8,128)(2,1)S(1)} copy-done((bf16[512,1152]{1,0:T(8,128)(2,1)S(1)}, bf16[512,1152]{1,0:T(8,128)(2,1)}, u32[]{:S(2)}) %copy-start) | copy-done | bytes 1179672
  1.9 0.0 copy-start.1
  1.9 1.3 %copy-done.1 = bf16[384,1536]{1,0:T(8,128)(2,1)S(1)} copy-done((bf16[384,1536]{1,0:T(8,128)(2,1)S(1)}, bf16[384,1536]{1,0:T(8,128)(2,1)}, u32[]{:S(2)}) %copy-start.1) | copy-done | bytes 1179672
  3.2 0.0 copy-start.2
  3.2 1.3 %copy-done.2 = bf16[1152,512]{1,0:T(8,128)(2,1)S(1)} copy-done((bf16[1152,512]{1,0:T(8,128)(2,1)S(1)}, bf16[1152,512]{1,0:T(8,128)(2,1)}, u32[]{:S(2)}) %copy-start.2) | copy-done | bytes 1179672
  4.5 0.0 copy-start.3
  4.5 1.3 %copy-done.3 = bf16[1536,384]{1,0:T(8,128)(2,1)S(1)} copy-done((bf16[1536,384]{1,0:T(8,128)(2,1)S(1)}, bf16[1536,384]{1,0:T(8,128)(2,1)}, u32[]{:S(2)}) %copy-start.3) | copy-done | bytes 1179672
  5.7 0.0 copy-start.4
  5.7 1.2 %copy-done.4 = bf16[384,1152]{1,0:T(8,128)(2,1)S(1)} copy-done((bf16[384,1152]{1,0:T(8,128)(2,1)S(1)}, bf16[384,1152]{1,0:T(8,128)(2,1)}, u32[]{:S(2)}) %copy-start.4) | copy-done | bytes 884760
  6.9 0.0 copy-start.5
  6.9 1.0 %copy-done.5 = f32[12,24,384]{2,1,0:T(8,128)S(1)} copy-done((f32[12,24,384]{2,1,0:T(8,128)S(1)}, f32[12,24,384]{2,1,0:T(8,128)}, u32[]{:S(2)}) %copy-start.5) | copy-done | bytes 442392
  7.9 0.0 copy-start.6
  7.9 1.0 %copy-done.6 = f32[2,384,128]{2,1,0:T(8,128)S(1)} copy-done((f32[2,384,128]{2,1,0:T(8,128)S(1)}, f32[2,384,128]{2,1,0:T(8,128)}, u32[]{:S(2)}) %copy-start.6) | copy-done | bytes 393240
  8.9 0.0 copy-start.7
  8.9 0.7 copy-done.7
  9.7 0.0 copy-start.8
  9.7 0.7 copy-done.8
  10.3 0.0 copy-start.9
  10.3 0.7 copy-done.9
  11.0 0.0 copy-start.10
  11.0 0.7 copy-done.10
  11.7 0.0 copy-start.11
  11.7 0.7 copy-done.11
  12.4 84.0 %ewald.1 = f32[3,1,1,256]{3,2,1,0:T(1,128)S(1)} custom-call(f32[1,1,256]{2,1,0:T(1,128)S(1)} %copy-done.8, f32[1,1,256]{2,1,0:T(1,128)S(1)} %copy-done.9, f32[1,1,256]{2,1,0:T(1,128)S(1)} %copy-done.10, f32[1,1,256]{2,1,0:T(1,128)S(1)} %copy-done.11, s32[1,1]{1,0:T(1,128)S(6)} %copy.15.counts, f32[12,24,384]{2,1,0:T(8,128)S(1)} %copy-done.5, ...), custom_call_target="tpu_custom_call" | custom-call | tf_op jit(solution)/shard_map/ewald/pallas_call | solution.py:512
  96.3 0.6 copy.16
Async XLA Ops:
  0.7 1.3 %copy-start = (bf16[512,1152]{1,0:T(8,128)(2,1)S(1)}, bf16[512,1152]{1,0:T(8,128)(2,1)}, u32[]{:S(2)}) copy-start(bf16[512,1152]{1,0:T(8,128)(2,1)} %constant.18.clone.back_x_hbm) | copy-start | bytes 3538948
  1.9 1.3 %copy-start.1 = (bf16[384,1536]{1,0:T(8,128)(2,1)S(1)}, bf16[384,1536]{1,0:T(8,128)(2,1)}, u32[]{:S(2)}) copy-start(bf16[384,1536]{1,0:T(8,128)(2,1)} %constant.17.clone.ahead_x_hbm) | copy-start | bytes 3538948
  3.2 1.3 %copy-start.2 = (bf16[1152,512]{1,0:T(8,128)(2,1)S(1)}, bf16[1152,512]{1,0:T(8,128)(2,1)}, u32[]{:S(2)}) copy-start(bf16[1152,512]{1,0:T(8,128)(2,1)} %constant.16.clone.back_y_hbm) | copy-start | bytes 3538948
  4.5 1.3 %copy-start.3 = (bf16[1536,384]{1,0:T(8,128)(2,1)S(1)}, bf16[1536,384]{1,0:T(8,128)(2,1)}, u32[]{:S(2)}) copy-start(bf16[1536,384]{1,0:T(8,128)(2,1)} %constant.15.clone.ahead_y_hbm) | copy-start | bytes 3538948
  5.7 1.2 %copy-start.4 = (bf16[384,1152]{1,0:T(8,128)(2,1)S(1)}, bf16[384,1152]{1,0:T(8,128)(2,1)}, u32[]{:S(2)}) copy-start(bf16[384,1152]{1,0:T(8,128)(2,1)} %constant.14.clone.table_z_hbm) | copy-start | bytes 2654212
  6.9 1.0 %copy-start.5 = (f32[12,24,384]{2,1,0:T(8,128)S(1)}, f32[12,24,384]{2,1,0:T(8,128)}, u32[]{:S(2)}) copy-start(f32[12,24,384]{2,1,0:T(8,128)} %background.1) | copy-start | bytes 1327108
  7.9 1.0 %copy-start.6 = (f32[2,384,128]{2,1,0:T(8,128)S(1)}, f32[2,384,128]{2,1,0:T(8,128)}, u32[]{:S(2)}) copy-start(f32[2,384,128]{2,1,0:T(8,128)} %constant.19.clone.green_x_hbm) | copy-start | bytes 1179652
  8.9 0.7 copy-start.7
  9.7 0.7 copy-start.8
  10.3 0.7 copy-start.9
  11.0 0.7 copy-start.10
  11.7 0.7 copy-start.11
where the time goes:
time: 97.4 us; the launch traced here: 96.9 us
  Pallas kernels  84 us (86%)
  local copies, waits for them, and re-layouts  12.3 us (13%)
    pallas_call x1, Pallas kernels, per_device(): pl.pallas_call(kernel, out_shape=jax.ShapeDtypeStruct((3, 1, 1, SLOTS), F...  84 us
    unnamed x25, local copies, waits for them, and re-layouts  12.3 us

commit v1 on v0

--- a/solution.py
+++ b/solution.py
@@ -125,12 +125,12 @@
 
 
 def kernel(
-    atom_x,
-    atom_y,
-    atom_z,
-    charges,
+    atom_x_hbm,
+    atom_y_hbm,
+    atom_z_hbm,
+    charges_hbm,
     counts,
-    background,
+    background_hbm,
     table_z_hbm,
     ahead_y_hbm,
     back_y_hbm,
@@ -139,6 +139,11 @@
     green_x_hbm,
     green_y_hbm,
     out,
+    atom_x,
+    atom_y,
+    atom_z,
+    charges,
+    background,
     table_z,
     ahead_y,
     back_y,
@@ -204,7 +209,12 @@
         pltpu.make_async_copy(source, target, table_sem.at[place])
         for place, (source, target) in enumerate(
             (
+                (atom_x_hbm, atom_x),
+                (atom_y_hbm, atom_y),
+                (atom_z_hbm, atom_z),
+                (charges_hbm, charges),
                 (table_z_hbm, table_z),
+                (background_hbm, background),
                 (ahead_y_hbm, ahead_y),
                 (ahead_x_hbm, ahead_x),
                 (green_x_hbm, green_x),
@@ -220,6 +230,8 @@
     wave_in[:, :, KX:, :] = jnp.zeros((3, RING, EX - KX, 128), F32)
     back_in[:, KX:, :] = jnp.zeros((UNITS, EX - KX, 128), F32)
 
+    for copy in tables[:4]:
+        copy.wait()
     slot = lax.broadcasted_iota(jnp.int32, (1, SLOTS), 1)
     live = jnp.where(slot < counts[0, 0], charges[0], 0.0)
     inner_y = lax.broadcasted_iota(jnp.int32, (EY, SLOTS), 0)
@@ -257,6 +269,7 @@
     mixed_parts[:, SLOTS : 2 * SLOTS] = high
     mixed_parts[:, 2 * SLOTS :] = low
 
+    tables[5].wait()
     for group in range(3):
         for y in range(CY):
             charge[group * 128 + y * 8 : group * 128 + y * 8 + 8, :] = background[
@@ -268,7 +281,7 @@
     charge_parts[:, N : 2 * N] = high
     charge_parts[:, 2 * N :] = low
 
-    tables[0].wait()
+    tables[4].wait()
     high, low = halves(dot(table_z[...], weight_z[...]))
     deposit_parts[:, :SLOTS] = high
     deposit_parts[:, SLOTS : 2 * SLOTS] = low
@@ -316,7 +329,7 @@
                 chunk * 128 : chunk * 128 + 128
             ]
 
-    tables[1].wait()
+    tables[6].wait()
     spread_got = spread_in.reshape(CHUNKS, 4, 128, 128)
 
     @pl.loop(0, CHUNKS)
@@ -362,7 +375,7 @@
                     wave_out.at[unit, 0:KX], wave_in.at[place, ring, 0:KX], recv_two.at[place]
                 ).start()
 
-    for copy in tables[2:6]:
+    for copy in tables[7:11]:
         copy.wait()
     base = lax.rem(13 * (ring + RING - 8 * core), RING)
     n_places = lax.div(UNITS - 1 - base, RING) + 1
@@ -403,7 +416,7 @@
                 device_id_type=MESH,
             ).start()
 
-    tables[6].wait()
+    tables[11].wait()
     cell_tiles = cell_out.reshape(CHUNKS, 4, 128, 128)
 
     @pl.loop(0, CHUNKS)
@@ -508,15 +521,15 @@
     def per_device(*args):
         vmem = pl.BlockSpec(memory_space=pltpu.VMEM)
         anywhere = pl.BlockSpec(memory_space=pl.ANY)
-        held = [pltpu.VMEM(tables[place].shape, tables[place].dtype) for place in range(7)]
+        held = [pltpu.VMEM(value.shape, value.dtype) for value in (*args[:4], args[5], *tables)]
         return pl.pallas_call(
             kernel,
             out_shape=jax.ShapeDtypeStruct((3, 1, 1, SLOTS), F32),
-            in_specs=[vmem] * 4 + [pl.BlockSpec(memory_space=pltpu.SMEM), vmem] + [anywhere] * 7,
+            in_specs=[anywhere] * 4 + [pl.BlockSpec(memory_space=pltpu.SMEM)] + [anywhere] * 8,
             out_specs=vmem,
             scratch_shapes=held
             + [
-                pltpu.SemaphoreType.DMA((7,)),
+                pltpu.SemaphoreType.DMA((12,)),
                 pltpu.VMEM((3 * N, SLOTS), BF16),
                 pltpu.VMEM((3 * N, SLOTS), BF16),
                 pltpu.VMEM((4 * 128, SLOTS), F32),
@@ -546,7 +559,7 @@
                 pltpu.SemaphoreType.DMA((CHUNKS,)),
             ],
             compiler_params=pltpu.CompilerParams(
-                collective_id=0, has_side_effects=True, vmem_limit_bytes=40 * 1024 * 1024
+                collective_id=0, has_side_effects=True, vmem_limit_bytes=60 * 1024 * 1024
             ),
             name="ewald",
         )(*args, *(jnp.asarray(table) for table in tables))

time: 97.4 us -> 86.6 us (0.89)
  local copies, waits for them, and re-layouts: 12.3 us -> 1.26 us
    unnamed x25 -> x1, local copies, waits for them, and re-layouts: 12.3 us -> 1.26 us
where the time goes in v1:
time: 86.6 us; the launch traced here: 86.5 us
  Pallas kernels  84.5 us (98%)
  local copies, waits for them, and re-layouts  1.26 us (1%)
    pallas_call x1, Pallas kernels, per_device(): pl.pallas_call(kernel, out_shape=jax.ShapeDtypeStruct((3, 1, 1, SLOTS), F...  84.5 us

profile of v1, /device:TPU:1, one launch (start us, length us, event | category | flops | bytes accessed | tf_op | source)
XLA Modules:
  0.0 86.5 jit_solution(13079663578646869675)
XLA Ops:
  0.7 84.5 %ewald.1 = f32[3,1,1,256]{3,2,1,0:T(1,128)} custom-call(f32[1,1,256]{2,1,0:T(1,128)} %atom_x_hbm.1, f32[1,1,256]{2,1,0:T(1,128)} %atom_y_hbm.1, f32[1,1,256]{2,1,0:T(1,128)} %atom_z_hbm.1, f32[1,1,256]{2,1,0:T(1,128)} %charges_hbm.1, s32[1,1]{1,0:T(1,128)S(6)} %copy.15.counts, f32[12,24,384]{2,1,0:T(8,128)} %background_hbm.1, ...), custom_call_target="tpu_custom_call" | custom-call | tf_op jit(solution)/shard_map/ewald/pallas_call | solution.py:525
  85.2 1.3 %copy.16 = f32[3,1,1,256]{3,2,1,0:T(1,128)} copy(f32[3,1,1,256]{3,2,1,0:T(1,128)} %ewald.1) | data formatting | bytes 6144

commit v2 on v1

--- a/solution.py
+++ b/solution.py
@@ -14,8 +14,10 @@
 RING = 16
 ROWS = 32
 CX, CY = N // RING, N // ROWS
-EX, EY = 32, 16
-KX = 28
+EY = 16
+GROUPS = CX // 8
+MAIN = GROUPS * 128
+EDGE = 64
 SLOTS = 256
 CHUNKS = 3
 UNITS = 36
@@ -47,19 +49,12 @@
 
 def make_tables():
     wave = np.arange(N)
-    along_z = wide_table(cas(wave, wave))
+    along = wide_table(cas(wave, wave))
     inner_y = np.arange(EY)
     inner_y = np.where(inner_y < CY + 2, inner_y, inner_y - EY)
     cell_y = (inner_y[:, None] + CY * np.arange(ROWS)[None, :]).reshape(-1) % N
     ahead_y = tall_table(cas(cell_y, wave))
     back_y = tall_table(cas(wave, cell_y))
-    inner_x = np.arange(EX)
-    used = np.tile(inner_x < KX, RING)
-    inner_x = np.where(inner_x < CX + 2, inner_x, inner_x - KX)
-    cell_x = (CX * np.arange(RING)[:, None] + inner_x[None, :]).reshape(-1) % N
-    matrix_x = cas(wave, cell_x) * used[None, :]
-    ahead_x = wide_table(matrix_x)
-    back_x = wide_table(matrix_x.T)
     signed = np.where(wave <= N // 2, wave, wave - N) / N
     angles = 2.0 * math.pi / N * wave
     modulus = (230.0 + 152.0 * np.cos(angles) + 2.0 * np.cos(2.0 * angles)) / 384.0
@@ -69,11 +64,9 @@
     green_y = np.stack([decay * factor, signed**2]).reshape(2, 3, 1, 128)
     green_y = np.broadcast_to(green_y, (2, 3, 8, 128))
     return (
-        along_z,
+        along,
         ahead_y,
         back_y,
-        ahead_x,
-        back_x,
         np.ascontiguousarray(green_x, dtype=np.float32),
         np.ascontiguousarray(green_y, dtype=np.float32),
     )
@@ -131,11 +124,9 @@
     charges_hbm,
     counts,
     background_hbm,
-    table_z_hbm,
+    table_hbm,
     ahead_y_hbm,
     back_y_hbm,
-    ahead_x_hbm,
-    back_x_hbm,
     green_x_hbm,
     green_y_hbm,
     out,
@@ -144,11 +135,9 @@
     atom_z,
     charges,
     background,
-    table_z,
+    table,
     ahead_y,
     back_y,
-    ahead_x,
-    back_x,
     green_x,
     green_y,
     table_sem,
@@ -170,6 +159,11 @@
     back_in,
     cell_out,
     cell_in,
+    halo_out,
+    halo_in,
+    flank_out,
+    flank_in,
+    cells,
     gathered,
     send_one,
     recv_one,
@@ -179,6 +173,10 @@
     recv_three,
     send_four,
     recv_four,
+    send_halo,
+    recv_halo,
+    send_flank,
+    recv_flank,
 ):
     ring = lax.axis_index("gx")
     major, minor = lax.axis_index("gy"), lax.axis_index("gz")
@@ -213,22 +211,17 @@
                 (atom_y_hbm, atom_y),
                 (atom_z_hbm, atom_z),
                 (charges_hbm, charges),
-                (table_z_hbm, table_z),
+                (table_hbm, table),
                 (background_hbm, background),
                 (ahead_y_hbm, ahead_y),
-                (ahead_x_hbm, ahead_x),
                 (green_x_hbm, green_x),
                 (green_y_hbm, green_y),
-                (back_x_hbm, back_x),
                 (back_y_hbm, back_y),
             )
         )
     ]
     for copy in tables:
         copy.start()
-
-    wave_in[:, :, KX:, :] = jnp.zeros((3, RING, EX - KX, 128), F32)
-    back_in[:, KX:, :] = jnp.zeros((UNITS, EX - KX, 128), F32)
 
     for copy in tables[:4]:
         copy.wait()
@@ -237,12 +230,9 @@
     inner_y = lax.broadcasted_iota(jnp.int32, (EY, SLOTS), 0)
     inner_y = jnp.where(inner_y < CY + 2, inner_y, inner_y - EY).astype(F32)
     height_y, slope_y = spline(atom_y[0] - inner_y + 2.5)
-    inner_x = lax.broadcasted_iota(jnp.int32, (EX, SLOTS), 0)
-    used = inner_x < KX
-    inner_x = jnp.where(inner_x < CX + 2, inner_x, inner_x - KX).astype(F32)
+    inner_x = lax.broadcasted_iota(jnp.int32, (CX + 8, SLOTS), 0)
+    inner_x = jnp.where(inner_x < CX + 2, inner_x, inner_x - CX - 4).astype(F32)
     height_x, slope_x = spline(atom_x[0] - inner_x + 2.5)
-    height_x = jnp.where(used, height_x, 0.0)
-    slope_x = jnp.where(used, slope_x, 0.0)
 
     @pl.loop(0, N // 64)
     def _(block):
@@ -259,30 +249,43 @@
             target[pl.ds(2 * N + first, 64), :] = low
 
     charged_y = height_y * live
+    for place in range(4):
+        mixed[MAIN + place * EY : MAIN + place * EY + EY, :] = (
+            height_x[CX + place : CX + place + 1] * charged_y
+        )
+    high, low = halves(mixed[MAIN:, :])
+    for side in range(2):
+        rows = slice(side * 32, side * 32 + 32)
+        halo_out[side] = (
+            dot_nt(high[rows], weight_z[:N, :])
+            + dot_nt(high[rows], weight_z[2 * N :, :])
+            + dot_nt(low[rows], weight_z[:N, :])
+        )
+
+    pl.semaphore_wait(barrier, ROWS - 1 + RING - 1)
+    sides = (lax.rem(ring + 1, RING), lax.rem(ring + RING - 1, RING))
+    for side in range(2):
+        pltpu.make_async_remote_copy(
+            halo_out.at[side],
+            halo_in.at[side],
+            send_halo.at[side],
+            recv_halo.at[side],
+            device_id=in_ring(sides[side]),
+            device_id_type=MESH,
+        ).start()
+
     for y in range(EY):
-        for group in range(4):
+        for group in range(GROUPS):
             mixed[group * 128 + y * 8 : group * 128 + y * 8 + 8, :] = (
                 height_x[group * 8 : group * 8 + 8] * charged_y[y : y + 1]
             )
-    high, low = halves(mixed[...])
+    high, low = halves(mixed[:MAIN, :])
     mixed_parts[:, :SLOTS] = high
     mixed_parts[:, SLOTS : 2 * SLOTS] = high
     mixed_parts[:, 2 * SLOTS :] = low
 
-    tables[5].wait()
-    for group in range(3):
-        for y in range(CY):
-            charge[group * 128 + y * 8 : group * 128 + y * 8 + 8, :] = background[
-                y, group * 8 : group * 8 + 8, :
-            ]
-        charge[group * 128 + CY * 8 : group * 128 + 128, :] = jnp.zeros((128 - CY * 8, N), F32)
-    high, low = halves(charge[...])
-    charge_parts[:, :N] = high
-    charge_parts[:, N : 2 * N] = high
-    charge_parts[:, 2 * N :] = low
-
     tables[4].wait()
-    high, low = halves(dot(table_z[...], weight_z[...]))
+    high, low = halves(dot(table[...], weight_z[...]))
     deposit_parts[:, :SLOTS] = high
     deposit_parts[:, SLOTS : 2 * SLOTS] = low
     deposit_parts[:, 2 * SLOTS :] = high
@@ -291,21 +294,44 @@
             pull_parts[chunk, place * 128 : place * 128 + 128, :SLOTS] = value[
                 chunk * 128 : chunk * 128 + 128
             ]
-
-    pl.semaphore_wait(barrier, ROWS - 1 + RING - 1)
-
-    spread_tiles = spread_out.reshape(CHUNKS, 4, 128, 128)
+    spread_tiles = spread_out.reshape(CHUNKS, GROUPS, 128, 128)
 
     @pl.loop(0, CHUNKS)
     def _(chunk):
         first = pl.multiple_of(chunk * 128, 128)
         atoms = dot_nt(deposit_parts[pl.ds(first, 128), :], mixed_parts[...])
-        frozen = dot_nt(table_z[pl.ds(first, 128), :], charge_parts[...])
-        for group in range(4):
-            tile = atoms[:, group * 128 : group * 128 + 128]
-            if group < 3:
-                tile = tile + frozen[:, group * 128 : group * 128 + 128]
-            spread_tiles[chunk, group] = tile
+        for group in range(GROUPS):
+            spread_tiles[chunk, group] = atoms[:, group * 128 : group * 128 + 128]
+
+    tables[5].wait()
+    for tile in range(3):
+        lanes = slice(tile * 128, tile * 128 + 128)
+        for group in range(GROUPS):
+            for y in range(CY):
+                charge[tile, group * 128 + y * 8 : group * 128 + y * 8 + 8, :] = background[
+                    y, group * 8 : group * 8 + 8, lanes
+                ]
+            charge[tile, group * 128 + CY * 8 : group * 128 + 128, :] = jnp.zeros(
+                (128 - CY * 8, 128), F32
+            )
+    for side, first in ((0, 0), (1, 2 * 128 + 6)):
+        pltpu.make_async_copy(halo_in.at[side], halo_in.at[side], recv_halo.at[side]).wait()
+        for place in range(2):
+            rows = pl.ds(first + place, EY, 8)
+            for tile in range(3):
+                lanes = slice(tile * 128, tile * 128 + 128)
+                charge[tile, rows, :] += halo_in[side, place * EY : place * EY + EY, lanes]
+    for tile in range(3):
+        high, low = halves(charge[tile])
+        for place, value in enumerate((high, high, low)):
+            charge_parts[:, place * N + tile * 128 : place * N + tile * 128 + 128] = value
+
+    @pl.loop(0, CHUNKS)
+    def _(chunk):
+        first = pl.multiple_of(chunk * 128, 128)
+        waves = dot_nt(table[pl.ds(first, 128), :], charge_parts[...])
+        for group in range(GROUPS):
+            spread_tiles[chunk, group] += waves[:, group * 128 : group * 128 + 128]
         pltpu.make_async_copy(
             spread_out.at[chunk, :, row], spread_in.at[chunk, :, :, row], recv_one.at[chunk]
         ).start()
@@ -322,7 +348,7 @@
                 device_id_type=MESH,
             ).start()
 
-    high, low = halves(dot(table_z[...], slope_z[...]))
+    high, low = halves(dot(table[...], slope_z[...]))
     for chunk in range(CHUNKS):
         for place, value in enumerate((high, low, high)):
             pull_parts[chunk, place * 128 : place * 128 + 128, SLOTS:] = value[
@@ -330,18 +356,18 @@
             ]
 
     tables[6].wait()
-    spread_got = spread_in.reshape(CHUNKS, 4, 128, 128)
+    spread_got = spread_in.reshape(CHUNKS, GROUPS, 128, 128)
 
     @pl.loop(0, CHUNKS)
     def _(chunk):
         pltpu.make_async_copy(spread_in.at[chunk], spread_in.at[chunk], recv_one.at[chunk]).wait()
-        for group in range(4):
+        for group in range(GROUPS):
             flipped = spread_got[chunk, group].T
             for quarter in range(4):
                 items = [flipped[(quarter * 4 + j) * 8 : (quarter * 4 + j) * 8 + 8] for j in range(4)]
                 for k, item in enumerate(exchange_blocks(items)):
                     lines[
-                        k * EX + group * 8 : k * EX + group * 8 + 8,
+                        k * CX + group * 8 : k * CX + group * 8 + 8,
                         quarter * 128 : quarter * 128 + 128,
                     ] = item
         high, low = halves(lines[...])
@@ -349,7 +375,7 @@
         for k in range(4):
             for tile in range(3):
                 wave_out[chunk * 12 + k * 3 + tile] = waves[
-                    k * EX : k * EX + EX, tile * 128 : tile * 128 + 128
+                    k * CX : k * CX + CX, tile * 128 : tile * 128 + 128
                 ]
 
         @pl.loop(0, 12)
@@ -361,8 +387,8 @@
             @pl.when(target != ring)
             def _():
                 pltpu.make_async_remote_copy(
-                    wave_out.at[unit, 0:KX],
-                    wave_in.at[place, ring, 0:KX],
+                    wave_out.at[unit],
+                    wave_in.at[place, ring],
                     send_two.at[unit],
                     recv_two.at[place],
                     device_id=in_ring(target),
@@ -372,10 +398,10 @@
             @pl.when(target == ring)
             def _():
                 pltpu.make_async_copy(
-                    wave_out.at[unit, 0:KX], wave_in.at[place, ring, 0:KX], recv_two.at[place]
+                    wave_out.at[unit], wave_in.at[place, ring], recv_two.at[place]
                 ).start()
 
-    for copy in tables[7:11]:
+    for copy in tables[7:9]:
         copy.wait()
     base = lax.rem(13 * (ring + RING - 8 * core), RING)
     n_places = lax.div(UNITS - 1 - base, RING) + 1
@@ -384,10 +410,10 @@
     def _(place):
         unit = place * RING + base
         pltpu.make_async_copy(
-            wave_in.at[place, :, 0:KX], wave_in.at[place, :, 0:KX], recv_two.at[place]
+            wave_in.at[place, :], wave_in.at[place, :], recv_two.at[place]
         ).wait()
-        high, low = halves(wave_in[place].reshape(RING * EX, 128))
-        waves = dot(ahead_x[...], jnp.concatenate([high, high, low], axis=0))
+        high, low = halves(wave_in[place].reshape(N, 128))
+        waves = dot(table[...], jnp.concatenate([high, high, low], axis=0))
         within = lax.rem(unit, 12)
         wave_z = lax.div(unit, 12) * 128 + row * 4 + lax.div(within, 3)
         tile = lax.rem(within, 3)
@@ -397,33 +423,33 @@
         decays = green_x[0].reshape(N // 8, 8, 128) * decay[None]
         green = jnp.where(squares > 0.0, decays / jnp.where(squares > 0.0, squares, 1.0), 0.0)
         high, low = halves(waves * green.reshape(N, 128))
-        cells = dot(back_x[...], jnp.concatenate([high, high, low], axis=0))
-        back_out[place] = cells.reshape(RING, EX, 128)
+        cells = dot(table[...], jnp.concatenate([high, high, low], axis=0))
+        back_out[place] = cells.reshape(RING, CX, 128)
         group = lax.div(unit, 12)
         pltpu.make_async_copy(
-            back_out.at[place, ring, 0:KX], back_in.at[unit, 0:KX], recv_three.at[group]
+            back_out.at[place, ring], back_in.at[unit], recv_three.at[group]
         ).start()
 
         @pl.loop(1, RING)
         def _(step):
             target = lax.rem(ring + step, RING)
             pltpu.make_async_remote_copy(
-                back_out.at[place, target, 0:KX],
-                back_in.at[unit, 0:KX],
+                back_out.at[place, target],
+                back_in.at[unit],
                 send_three.at[place, target],
                 recv_three.at[group],
                 device_id=in_ring(target),
                 device_id_type=MESH,
             ).start()
 
-    tables[11].wait()
-    cell_tiles = cell_out.reshape(CHUNKS, 4, 128, 128)
+    tables[9].wait()
+    cell_tiles = cell_out.reshape(CHUNKS, GROUPS, 128, 128)
 
     @pl.loop(0, CHUNKS)
     def _(chunk):
         units = pl.ds(chunk * 12, 12)
         pltpu.make_async_copy(
-            back_in.at[units, 0:KX], back_in.at[units, 0:KX], recv_three.at[chunk]
+            back_in.at[units], back_in.at[units], recv_three.at[chunk]
         ).wait()
         tiles = [
             jnp.concatenate([back_in[chunk * 12 + k * 3 + tile] for tile in range(3)], axis=1)
@@ -431,11 +457,11 @@
         ]
         high, low = halves(jnp.concatenate(tiles, axis=0))
         lines[...] = dot(jnp.concatenate([high, high, low], axis=1), back_y[...])
-        for group in range(4):
+        for group in range(GROUPS):
             for quarter in range(4):
                 items = [
                     lines[
-                        k * EX + group * 8 : k * EX + group * 8 + 8,
+                        k * CX + group * 8 : k * CX + group * 8 + 8,
                         quarter * 128 : quarter * 128 + 128,
                     ]
                     for k in range(4)
@@ -459,17 +485,38 @@
                 device_id_type=MESH,
             ).start()
 
-    cell_got = cell_in.reshape(CHUNKS, 4, 128, 128)
-    gathered[...] = jnp.zeros((4 * 128, 2 * SLOTS), F32)
+    cell_got = cell_in.reshape(CHUNKS, GROUPS, 128, 128)
+    gathered[...] = jnp.zeros((MAIN + EDGE, 2 * SLOTS), F32)
 
     @pl.loop(0, CHUNKS)
     def _(chunk):
         pltpu.make_async_copy(cell_in.at[chunk], cell_in.at[chunk], recv_four.at[chunk]).wait()
-        for group in range(4):
-            high, low = halves(cell_got[chunk, group].T)
-            gathered[group * 128 : group * 128 + 128, :] += dot(
-                jnp.concatenate([high, high, low], axis=1), pull_parts[chunk]
-            )
+        for group in range(GROUPS):
+            cells[group * 128 : group * 128 + 128, :] = cell_got[chunk, group].T
+        for side, first in ((0, 2 * 128 + 6), (1, 0)):
+            for place in range(2):
+                flank_out[chunk, side, place * EY : place * EY + EY, :] = cells[
+                    pl.ds(first + place, EY, 8), :
+                ]
+            pltpu.make_async_remote_copy(
+                flank_out.at[chunk, side],
+                flank_in.at[chunk, side],
+                send_flank.at[chunk, side],
+                recv_flank.at[chunk, side],
+                device_id=in_ring(sides[side]),
+                device_id_type=MESH,
+            ).start()
+        high, low = halves(cells[...])
+        gathered[:MAIN, :] += dot(jnp.concatenate([high, high, low], axis=1), pull_parts[chunk])
+
+    @pl.loop(0, CHUNKS)
+    def _(chunk):
+        for side in range(2):
+            pltpu.make_async_copy(
+                flank_in.at[chunk, side], flank_in.at[chunk, side], recv_flank.at[chunk, side]
+            ).wait()
+        high, low = halves(flank_in[chunk].reshape(EDGE, 128))
+        gathered[MAIN:, :] += dot(jnp.concatenate([high, high, low], axis=1), pull_parts[chunk])
 
     force_x = jnp.zeros((8, SLOTS), F32)
     force_y = jnp.zeros((8, SLOTS), F32)
@@ -478,7 +525,7 @@
         along_x = jnp.zeros((8, SLOTS), F32)
         turned_x = jnp.zeros((8, SLOTS), F32)
         depth_x = jnp.zeros((8, SLOTS), F32)
-        for group in range(4):
+        for group in range(GROUPS):
             first = group * 128 + y * 8
             plain = gathered[first : first + 8, :SLOTS]
             deriv = gathered[first : first + 8, SLOTS:]
@@ -489,8 +536,26 @@
         force_x += height_y[y : y + 1] * turned_x
         force_y += slope_y[y : y + 1] * along_x
         force_z += height_y[y : y + 1] * depth_x
+    for half in range(2):
+        along_x = jnp.zeros((8, SLOTS), F32)
+        turned_x = jnp.zeros((8, SLOTS), F32)
+        depth_x = jnp.zeros((8, SLOTS), F32)
+        for place, x in enumerate((CX + 2, CX + 3, CX, CX + 1)):
+            first = MAIN + place * EY + half * 8
+            plain = gathered[first : first + 8, :SLOTS]
+            deriv = gathered[first : first + 8, SLOTS:]
+            along_x += height_x[x : x + 1] * plain
+            turned_x += slope_x[x : x + 1] * plain
+            depth_x += height_x[x : x + 1] * deriv
+        height = height_y[half * 8 : half * 8 + 8]
+        force_x += height * turned_x
+        force_y += slope_y[half * 8 : half * 8 + 8] * along_x
+        force_z += height * depth_x
     for place, force in enumerate((force_x, force_y, force_z)):
         out[place, 0] = -live * jnp.sum(force, axis=0, keepdims=True)
+
+    for side in range(2):
+        pltpu.make_async_copy(halo_out.at[side], halo_out.at[side], send_halo.at[side]).wait()
 
     @pl.loop(0, CHUNKS)
     def _(chunk):
@@ -498,12 +563,15 @@
         pltpu.make_async_copy(sizes, sizes, send_one.at[chunk]).wait()
         sizes = cell_in.at[chunk, :, 0 : ROWS - 1]
         pltpu.make_async_copy(sizes, sizes, send_four.at[chunk]).wait()
+        for side in range(2):
+            sizes = flank_out.at[chunk, side]
+            pltpu.make_async_copy(sizes, sizes, send_flank.at[chunk, side]).wait()
 
     @pl.loop(0, UNITS)
     def _(unit):
         @pl.when(lax.rem(5 * unit + 8 * core, RING) != ring)
         def _():
-            sizes = wave_out.at[unit, 0:KX]
+            sizes = wave_out.at[unit]
             pltpu.make_async_copy(sizes, sizes, send_two.at[unit]).wait()
 
     @pl.loop(0, n_places)
@@ -511,7 +579,7 @@
         @pl.loop(1, RING)
         def _(step):
             target = lax.rem(ring + step, RING)
-            sizes = back_out.at[place, target, 0:KX]
+            sizes = back_out.at[place, target]
             pltpu.make_async_copy(sizes, sizes, send_three.at[place, target]).wait()
 
 
@@ -525,30 +593,35 @@
         return pl.pallas_call(
             kernel,
             out_shape=jax.ShapeDtypeStruct((3, 1, 1, SLOTS), F32),
-            in_specs=[anywhere] * 4 + [pl.BlockSpec(memory_space=pltpu.SMEM)] + [anywhere] * 8,
+            in_specs=[anywhere] * 4 + [pl.BlockSpec(memory_space=pltpu.SMEM)] + [anywhere] * 6,
             out_specs=vmem,
             scratch_shapes=held
             + [
-                pltpu.SemaphoreType.DMA((12,)),
+                pltpu.SemaphoreType.DMA((10,)),
                 pltpu.VMEM((3 * N, SLOTS), BF16),
                 pltpu.VMEM((3 * N, SLOTS), BF16),
-                pltpu.VMEM((4 * 128, SLOTS), F32),
-                pltpu.VMEM((4 * 128, 3 * SLOTS), BF16),
-                pltpu.VMEM((3 * 128, N), F32),
-                pltpu.VMEM((3 * 128, 3 * N), BF16),
+                pltpu.VMEM((MAIN + EDGE, SLOTS), F32),
+                pltpu.VMEM((MAIN, 3 * SLOTS), BF16),
+                pltpu.VMEM((3, MAIN, 128), F32),
+                pltpu.VMEM((MAIN, 3 * N), BF16),
                 pltpu.VMEM((N, 3 * SLOTS), BF16),
                 pltpu.VMEM((CHUNKS, 3 * 128, 2 * SLOTS), BF16),
-                pltpu.VMEM((4 * EX, EY * ROWS), F32),
+                pltpu.VMEM((4 * CX, EY * ROWS), F32),
                 pltpu.VMEM((128, 128), F32),
-                pltpu.VMEM((CHUNKS, 4, ROWS, 4, 1, 128), F32),
-                pltpu.VMEM((CHUNKS, 4, 4, ROWS, 1, 128), F32),
-                pltpu.VMEM((UNITS, EX, 128), F32),
-                pltpu.VMEM((3, RING, EX, 128), F32),
-                pltpu.VMEM((3, RING, EX, 128), F32),
-                pltpu.VMEM((UNITS, EX, 128), F32),
-                pltpu.VMEM((CHUNKS, 4, 4, ROWS, 1, 128), F32),
-                pltpu.VMEM((CHUNKS, 4, ROWS, 4, 1, 128), F32),
-                pltpu.VMEM((4 * 128, 2 * SLOTS), F32),
+                pltpu.VMEM((CHUNKS, GROUPS, ROWS, 4, 1, 128), F32),
+                pltpu.VMEM((CHUNKS, GROUPS, 4, ROWS, 1, 128), F32),
+                pltpu.VMEM((UNITS, CX, 128), F32),
+                pltpu.VMEM((3, RING, CX, 128), F32),
+                pltpu.VMEM((3, RING, CX, 128), F32),
+                pltpu.VMEM((UNITS, CX, 128), F32),
+                pltpu.VMEM((CHUNKS, GROUPS, 4, ROWS, 1, 128), F32),
+                pltpu.VMEM((CHUNKS, GROUPS, ROWS, 4, 1, 128), F32),
+                pltpu.VMEM((2, 32, N), F32),
+                pltpu.VMEM((2, 32, N), F32),
+                pltpu.VMEM((CHUNKS, 2, 32, 128), F32),
+                pltpu.VMEM((CHUNKS, 2, 32, 128), F32),
+                pltpu.VMEM((MAIN, 128), F32),
+                pltpu.VMEM((MAIN + EDGE, 2 * SLOTS), F32),
                 pltpu.SemaphoreType.DMA((CHUNKS,)),
                 pltpu.SemaphoreType.DMA((CHUNKS,)),
                 pltpu.SemaphoreType.DMA((UNITS,)),
@@ -557,6 +630,10 @@
                 pltpu.SemaphoreType.DMA((CHUNKS,)),
                 pltpu.SemaphoreType.DMA((CHUNKS,)),
                 pltpu.SemaphoreType.DMA((CHUNKS,)),
+                pltpu.SemaphoreType.DMA((2,)),
+                pltpu.SemaphoreType.DMA((2,)),
+                pltpu.SemaphoreType.DMA((CHUNKS, 2)),
+                pltpu.SemaphoreType.DMA((CHUNKS, 2)),
             ],
             compiler_params=pltpu.CompilerParams(
                 collective_id=0, has_side_effects=True, vmem_limit_bytes=60 * 1024 * 1024

time: 86.6 us -> 84.8 us (0.979)
  Pallas kernels: 84.5 us -> 82.7 us
    pallas_call x1, Pallas kernels: 84.5 us -> 82.7 us  [per_device(): pl.pallas_call(kernel, out_shape=jax.ShapeDtypeStruct((3, 1, 1, SLOTS), F...]
where the time goes in v2:
time: 84.8 us; the launch traced here: 84.6 us
  Pallas kernels  82.7 us (98%)
  local copies, waits for them, and re-layouts  1.26 us (1%)
    pallas_call x1, Pallas kernels, per_device(): pl.pallas_call(kernel, out_shape=jax.ShapeDtypeStruct((3, 1, 1, SLOTS), F...  82.7 us

profile of v2, /device:TPU:1, one launch (start us, length us, event | category | flops | bytes accessed | tf_op | source)
XLA Modules:
  0.0 84.6 jit_solution(15437631514070028617)
XLA Ops:
  0.7 82.7 %ewald.1 = f32[3,1,1,256]{3,2,1,0:T(1,128)} custom-call(f32[1,1,256]{2,1,0:T(1,128)} %atom_x_hbm.1, f32[1,1,256]{2,1,0:T(1,128)} %atom_y_hbm.1, f32[1,1,256]{2,1,0:T(1,128)} %atom_z_hbm.1, f32[1,1,256]{2,1,0:T(1,128)} %charges_hbm.1, s32[1,1]{1,0:T(1,128)S(6)} %copy.13.counts, f32[12,24,384]{2,1,0:T(8,128)} %background_hbm.1, ...), custom_call_target="tpu_custom_call" | custom-call | tf_op jit(solution)/shard_map/ewald/pallas_call | solution.py:593
  83.4 1.3 %copy.14 = f32[3,1,1,256]{3,2,1,0:T(1,128)} copy(f32[3,1,1,256]{3,2,1,0:T(1,128)} %ewald.1) | data formatting | bytes 6144

commit v3 on v2

--- a/solution.py
+++ b/solution.py
@@ -326,12 +326,7 @@
         for place, value in enumerate((high, high, low)):
             charge_parts[:, place * N + tile * 128 : place * N + tile * 128 + 128] = value
 
-    @pl.loop(0, CHUNKS)
-    def _(chunk):
-        first = pl.multiple_of(chunk * 128, 128)
-        waves = dot_nt(table[pl.ds(first, 128), :], charge_parts[...])
-        for group in range(GROUPS):
-            spread_tiles[chunk, group] += waves[:, group * 128 : group * 128 + 128]
+    def post_lines(chunk):
         pltpu.make_async_copy(
             spread_out.at[chunk, :, row], spread_in.at[chunk, :, :, row], recv_one.at[chunk]
         ).start()
@@ -348,12 +343,37 @@
                 device_id_type=MESH,
             ).start()
 
-    high, low = halves(dot(table[...], slope_z[...]))
-    for chunk in range(CHUNKS):
-        for place, value in enumerate((high, low, high)):
-            pull_parts[chunk, place * 128 : place * 128 + 128, SLOTS:] = value[
-                chunk * 128 : chunk * 128 + 128
-            ]
+    def lines_left(chunk):
+        sizes = spread_out.at[chunk, :, 0 : ROWS - 1]
+        pltpu.make_async_copy(sizes, sizes, send_one.at[chunk]).wait()
+
+    @pl.loop(0, CHUNKS)
+    def _(chunk):
+        first = pl.multiple_of(chunk * 128, 128)
+        waves = dot_nt(table[pl.ds(first, 128), :], charge_parts[...])
+        for group in range(GROUPS):
+            spread_tiles[chunk, group] += waves[:, group * 128 : group * 128 + 128]
+
+        @pl.when(chunk == 0)
+        def _():
+            post_lines(0)
+
+    lines_left(0)
+    post_lines(1)
+
+    def wave_left(unit):
+        @pl.when(lax.rem(5 * unit + 8 * core, RING) != ring)
+        def _():
+            pltpu.make_async_copy(wave_out.at[unit], wave_out.at[unit], send_two.at[unit]).wait()
+
+    def far_first(step):
+        half = lax.div(step, 2)
+        return lax.rem(ring + RING // 2 + jnp.where(lax.rem(step, 2) == 1, half, -half), RING)
+
+    def cells_left(place, step):
+        target = far_first(step)
+        sent = back_out.at[place, target]
+        pltpu.make_async_copy(sent, sent, send_three.at[place, target]).wait()
 
     tables[6].wait()
     spread_got = spread_in.reshape(CHUNKS, GROUPS, 128, 128)
@@ -378,13 +398,18 @@
                     k * CX : k * CX + CX, tile * 128 : tile * 128 + 128
                 ]
 
-        @pl.loop(0, 12)
+        @pl.loop(1, RING + 1)
         def _(step):
-            unit = chunk * 12 + lax.rem(step + lax.div(3 * ring, 4), 12)
-            target = lax.rem(5 * unit + 8 * core, RING)
+            target = far_first(step)
+            within = lax.rem(13 * (target + RING - 8 * core) + RING * 12 - chunk * 12, RING)
+            unit = chunk * 12 + within
             place = lax.div(unit, RING)
 
-            @pl.when(target != ring)
+            @pl.when((chunk > 0) & (within < 12))
+            def _():
+                wave_left(unit - 12)
+
+            @pl.when((target != ring) & (within < 12))
             def _():
                 pltpu.make_async_remote_copy(
                     wave_out.at[unit],
@@ -395,11 +420,23 @@
                     device_id_type=MESH,
                 ).start()
 
-            @pl.when(target == ring)
+            @pl.when((target == ring) & (within < 12))
             def _():
                 pltpu.make_async_copy(
                     wave_out.at[unit], wave_in.at[place, ring], recv_two.at[place]
                 ).start()
+
+        @pl.when(chunk == 0)
+        def _():
+            lines_left(1)
+            post_lines(2)
+
+    high, low = halves(dot(table[...], slope_z[...]))
+    for chunk in range(CHUNKS):
+        for place, value in enumerate((high, low, high)):
+            pull_parts[chunk, place * 128 : place * 128 + 128, SLOTS:] = value[
+                chunk * 128 : chunk * 128 + 128
+            ]
 
     for copy in tables[7:9]:
         copy.wait()
@@ -432,7 +469,16 @@
 
         @pl.loop(1, RING)
         def _(step):
-            target = lax.rem(ring + step, RING)
+            target = far_first(step)
+
+            @pl.when((place == 0) & (step <= 12))
+            def _():
+                wave_left(24 + lax.rem(step - 1 + lax.div(3 * ring, 4), 12))
+
+            @pl.when(place > 0)
+            def _():
+                cells_left(place - 1, step)
+
             pltpu.make_async_remote_copy(
                 back_out.at[place, target],
                 back_in.at[unit],
@@ -509,15 +555,6 @@
         high, low = halves(cells[...])
         gathered[:MAIN, :] += dot(jnp.concatenate([high, high, low], axis=1), pull_parts[chunk])
 
-    @pl.loop(0, CHUNKS)
-    def _(chunk):
-        for side in range(2):
-            pltpu.make_async_copy(
-                flank_in.at[chunk, side], flank_in.at[chunk, side], recv_flank.at[chunk, side]
-            ).wait()
-        high, low = halves(flank_in[chunk].reshape(EDGE, 128))
-        gathered[MAIN:, :] += dot(jnp.concatenate([high, high, low], axis=1), pull_parts[chunk])
-
     force_x = jnp.zeros((8, SLOTS), F32)
     force_y = jnp.zeros((8, SLOTS), F32)
     force_z = jnp.zeros((8, SLOTS), F32)
@@ -536,6 +573,15 @@
         force_x += height_y[y : y + 1] * turned_x
         force_y += slope_y[y : y + 1] * along_x
         force_z += height_y[y : y + 1] * depth_x
+    @pl.loop(0, CHUNKS)
+    def _(chunk):
+        for side in range(2):
+            pltpu.make_async_copy(
+                flank_in.at[chunk, side], flank_in.at[chunk, side], recv_flank.at[chunk, side]
+            ).wait()
+        high, low = halves(flank_in[chunk].reshape(EDGE, 128))
+        gathered[MAIN:, :] += dot(jnp.concatenate([high, high, low], axis=1), pull_parts[chunk])
+
     for half in range(2):
         along_x = jnp.zeros((8, SLOTS), F32)
         turned_x = jnp.zeros((8, SLOTS), F32)
@@ -554,33 +600,21 @@
     for place, force in enumerate((force_x, force_y, force_z)):
         out[place, 0] = -live * jnp.sum(force, axis=0, keepdims=True)
 
+    lines_left(2)
     for side in range(2):
         pltpu.make_async_copy(halo_out.at[side], halo_out.at[side], send_halo.at[side]).wait()
 
     @pl.loop(0, CHUNKS)
     def _(chunk):
-        sizes = spread_out.at[chunk, :, 0 : ROWS - 1]
-        pltpu.make_async_copy(sizes, sizes, send_one.at[chunk]).wait()
         sizes = cell_in.at[chunk, :, 0 : ROWS - 1]
         pltpu.make_async_copy(sizes, sizes, send_four.at[chunk]).wait()
         for side in range(2):
             sizes = flank_out.at[chunk, side]
             pltpu.make_async_copy(sizes, sizes, send_flank.at[chunk, side]).wait()
 
-    @pl.loop(0, UNITS)
-    def _(unit):
-        @pl.when(lax.rem(5 * unit + 8 * core, RING) != ring)
-        def _():
-            sizes = wave_out.at[unit]
-            pltpu.make_async_copy(sizes, sizes, send_two.at[unit]).wait()
-
-    @pl.loop(0, n_places)
-    def _(place):
-        @pl.loop(1, RING)
-        def _(step):
-            target = lax.rem(ring + step, RING)
-            sizes = back_out.at[place, target]
-            pltpu.make_async_copy(sizes, sizes, send_three.at[place, target]).wait()
+    @pl.loop(1, RING)
+    def _(step):
+        cells_left(n_places - 1, step)
 
 
 def solution(mesh):

time: 84.8 us -> 83.4 us (0.983)
  Pallas kernels: 82.7 us -> 81.3 us
    pallas_call x1, Pallas kernels: 82.7 us -> 81.3 us  [per_device(): pl.pallas_call(kernel, out_shape=jax.ShapeDtypeStruct((3, 1, 1, SLOTS), F...]
where the time goes in v3:
time: 83.4 us; the launch traced here: 83.2 us
  Pallas kernels  81.3 us (97%)
  local copies, waits for them, and re-layouts  1.26 us (2%)
    pallas_call x1, Pallas kernels, per_device(): pl.pallas_call(kernel, out_shape=jax.ShapeDtypeStruct((3, 1, 1, SLOTS), F...  81.3 us

profile of v3, /device:TPU:1, one launch (start us, length us, event | category | flops | bytes accessed | tf_op | source)
XLA Modules:
  0.0 83.2 jit_solution(684219174259705183)
XLA Ops:
  0.7 81.3 %ewald.1 = f32[3,1,1,256]{3,2,1,0:T(1,128)} custom-call(f32[1,1,256]{2,1,0:T(1,128)} %atom_x_hbm.1, f32[1,1,256]{2,1,0:T(1,128)} %atom_y_hbm.1, f32[1,1,256]{2,1,0:T(1,128)} %atom_z_hbm.1, f32[1,1,256]{2,1,0:T(1,128)} %charges_hbm.1, s32[1,1]{1,0:T(1,128)S(6)} %copy.13.counts, f32[12,24,384]{2,1,0:T(8,128)} %background_hbm.1, ...), custom_call_target="tpu_custom_call" | custom-call | tf_op jit(solution)/shard_map/ewald/pallas_call | solution.py:627
  82.0 1.3 %copy.14 = f32[3,1,1,256]{3,2,1,0:T(1,128)} copy(f32[3,1,1,256]{3,2,1,0:T(1,128)} %ewald.1) | data formatting | bytes 6144

commit v4 on v3

--- a/solution.py
+++ b/solution.py
@@ -72,19 +72,24 @@
     )
 
 
+def ramps(offset):
+    distance = jnp.minimum(offset, 5.0 - offset)
+    return (
+        jnp.maximum(distance, 0.0),
+        jnp.maximum(distance - 1.0, 0.0),
+        jnp.maximum(distance - 2.0, 0.0),
+    )
+
+
 def spline(offset):
-    distance = jnp.minimum(offset, 5.0 - offset)
-    ramp_zero = jnp.maximum(distance, 0.0)
-    ramp_one = jnp.maximum(distance - 1.0, 0.0)
-    ramp_two = jnp.maximum(distance - 2.0, 0.0)
-    cube_zero = ramp_zero * ramp_zero * ramp_zero
-    cube_one = ramp_one * ramp_one * ramp_one
-    cube_two = ramp_two * ramp_two * ramp_two
-    height = (cube_zero * ramp_zero - 5.0 * cube_one * ramp_one + 10.0 * cube_two * ramp_two) * (
-        1.0 / 24.0
-    )
-    gradient = (cube_zero - 5.0 * cube_one + 10.0 * cube_two) * (1.0 / 6.0)
-    return height, jnp.where(offset < 2.5, gradient, -gradient)
+    zero, one, two = (ramp * ramp for ramp in ramps(offset))
+    return (zero * zero - 5.0 * (one * one) + 10.0 * (two * two)) * (1.0 / 24.0)
+
+
+def spline_slope(offset):
+    zero, one, two = (ramp * ramp * ramp for ramp in ramps(offset))
+    slope = (zero - 5.0 * one + 10.0 * two) * (1.0 / 6.0)
+    return jnp.where(offset < 2.5, slope, -slope)
 
 
 def halves(value):
@@ -147,7 +152,6 @@
     mixed_parts,
     charge,
     charge_parts,
-    deposit_parts,
     pull_parts,
     lines,
     turned,
@@ -191,17 +195,35 @@
 
     barrier = pltpu.get_barrier_semaphore()
 
-    @pl.loop(1, ROWS)
-    def _(step):
-        pl.semaphore_signal(
-            barrier, inc=1, device_id=in_rows(lax.rem(row + step, ROWS)), device_id_type=MESH
-        )
+    def far_first(step, size):
+        half = lax.div(step, 2)
+        return size // 2 + jnp.where(lax.rem(step, 2) == 1, half, -half)
+
+    def ring_target(step):
+        return lax.rem(ring + far_first(step, RING), RING)
+
+    chip_x = 2 * lax.div(minor, 2) + lax.div(major, 4)
+    chip_y = lax.rem(major, 4)
+
+    def row_target(step):
+        x = lax.rem(chip_x + far_first(lax.div(step, 8) + 1, 4), 4)
+        y = lax.rem(chip_y + far_first(lax.rem(lax.div(step, 2), 4) + 1, 4), 4)
+        other = lax.rem(core + step, 2)
+        return (4 * lax.rem(x, 2) + y) * 4 + 2 * lax.div(x, 2) + other
 
     @pl.loop(1, RING)
     def _(step):
         pl.semaphore_signal(
-            barrier, inc=1, device_id=in_ring(lax.rem(ring + step, RING)), device_id_type=MESH
+            barrier, inc=1, device_id=in_ring(ring_target(step)), device_id_type=MESH
         )
+
+    @pl.loop(0, ROWS)
+    def _(step):
+        @pl.when(step != ROWS - 2)
+        def _():
+            pl.semaphore_signal(
+                barrier, inc=1, device_id=in_rows(row_target(step)), device_id_type=MESH
+            )
 
     tables = [
         pltpu.make_async_copy(source, target, table_sem.at[place])
@@ -229,25 +251,27 @@
     live = jnp.where(slot < counts[0, 0], charges[0], 0.0)
     inner_y = lax.broadcasted_iota(jnp.int32, (EY, SLOTS), 0)
     inner_y = jnp.where(inner_y < CY + 2, inner_y, inner_y - EY).astype(F32)
-    height_y, slope_y = spline(atom_y[0] - inner_y + 2.5)
+    offset_y = atom_y[0] - inner_y + 2.5
+    height_y = spline(offset_y)
     inner_x = lax.broadcasted_iota(jnp.int32, (CX + 8, SLOTS), 0)
     inner_x = jnp.where(inner_x < CX + 2, inner_x, inner_x - CX - 4).astype(F32)
-    height_x, slope_x = spline(atom_x[0] - inner_x + 2.5)
-
-    @pl.loop(0, N // 64)
-    def _(block):
-        first = pl.multiple_of(block * 64, 64)
-        plane = (lax.broadcasted_iota(jnp.int32, (64, SLOTS), 0) + first).astype(F32)
-        offset = atom_z[0] - plane
-        offset = jnp.where(offset >= N / 2.0, offset - N, offset)
-        offset = jnp.where(offset < -N / 2.0, offset + N, offset)
-        height, slope = spline(offset + 2.5)
-        for value, target in ((height, weight_z), (slope, slope_z)):
-            high, low = halves(value)
+    offset_x = atom_x[0] - inner_x + 2.5
+    height_x = spline(offset_x)
+
+    def fill_z(function, target):
+        @pl.loop(0, N // 64)
+        def _(block):
+            first = pl.multiple_of(block * 64, 64)
+            plane = (lax.broadcasted_iota(jnp.int32, (64, SLOTS), 0) + first).astype(F32)
+            offset = atom_z[0] - plane
+            offset = jnp.where(offset >= N / 2.0, offset - N, offset)
+            offset = jnp.where(offset < -N / 2.0, offset + N, offset)
+            high, low = halves(function(offset + 2.5))
             target[pl.ds(first, 64), :] = high
             target[pl.ds(N + first, 64), :] = high
             target[pl.ds(2 * N + first, 64), :] = low
 
+    fill_z(spline, weight_z)
     charged_y = height_y * live
     for place in range(4):
         mixed[MAIN + place * EY : MAIN + place * EY + EY, :] = (
@@ -285,23 +309,18 @@
     mixed_parts[:, 2 * SLOTS :] = low
 
     tables[4].wait()
-    high, low = halves(dot(table[...], weight_z[...]))
-    deposit_parts[:, :SLOTS] = high
-    deposit_parts[:, SLOTS : 2 * SLOTS] = low
-    deposit_parts[:, 2 * SLOTS :] = high
-    for chunk in range(CHUNKS):
+    spread_tiles = spread_out.reshape(CHUNKS, GROUPS, 128, 128)
+
+    def deposit(chunk):
+        first = pl.multiple_of(chunk * 128, 128)
+        high, low = halves(dot(table[pl.ds(first, 128), :], weight_z[...]))
         for place, value in enumerate((high, low, high)):
-            pull_parts[chunk, place * 128 : place * 128 + 128, :SLOTS] = value[
-                chunk * 128 : chunk * 128 + 128
-            ]
-    spread_tiles = spread_out.reshape(CHUNKS, GROUPS, 128, 128)
-
-    @pl.loop(0, CHUNKS)
-    def _(chunk):
-        first = pl.multiple_of(chunk * 128, 128)
-        atoms = dot_nt(deposit_parts[pl.ds(first, 128), :], mixed_parts[...])
+            pull_parts[chunk, place * 128 : place * 128 + 128, :SLOTS] = value
+        atoms = dot_nt(jnp.concatenate([high, low, high], axis=1), mixed_parts[...])
         for group in range(GROUPS):
             spread_tiles[chunk, group] = atoms[:, group * 128 : group * 128 + 128]
+
+    deposit(0)
 
     tables[5].wait()
     for tile in range(3):
@@ -331,32 +350,38 @@
             spread_out.at[chunk, :, row], spread_in.at[chunk, :, :, row], recv_one.at[chunk]
         ).start()
 
-        @pl.loop(1, ROWS)
+        @pl.loop(0, ROWS)
         def _(step):
-            target = lax.rem(row + step, ROWS)
-            pltpu.make_async_remote_copy(
-                spread_out.at[chunk, :, target],
-                spread_in.at[chunk, :, :, row],
-                send_one.at[chunk],
-                recv_one.at[chunk],
-                device_id=in_rows(target),
-                device_id_type=MESH,
-            ).start()
+            target = row_target(step)
+
+            @pl.when(step != ROWS - 2)
+            def _():
+                pltpu.make_async_remote_copy(
+                    spread_out.at[chunk, :, target],
+                    spread_in.at[chunk, :, :, row],
+                    send_one.at[chunk],
+                    recv_one.at[chunk],
+                    device_id=in_rows(target),
+                    device_id_type=MESH,
+                ).start()
 
     def lines_left(chunk):
         sizes = spread_out.at[chunk, :, 0 : ROWS - 1]
         pltpu.make_async_copy(sizes, sizes, send_one.at[chunk]).wait()
 
-    @pl.loop(0, CHUNKS)
-    def _(chunk):
+    def add_frozen(chunk):
         first = pl.multiple_of(chunk * 128, 128)
         waves = dot_nt(table[pl.ds(first, 128), :], charge_parts[...])
         for group in range(GROUPS):
             spread_tiles[chunk, group] += waves[:, group * 128 : group * 128 + 128]
 
-        @pl.when(chunk == 0)
-        def _():
-            post_lines(0)
+    add_frozen(0)
+    post_lines(0)
+
+    @pl.loop(1, CHUNKS)
+    def _(chunk):
+        deposit(chunk)
+        add_frozen(chunk)
 
     lines_left(0)
     post_lines(1)
@@ -366,12 +391,8 @@
         def _():
             pltpu.make_async_copy(wave_out.at[unit], wave_out.at[unit], send_two.at[unit]).wait()
 
-    def far_first(step):
-        half = lax.div(step, 2)
-        return lax.rem(ring + RING // 2 + jnp.where(lax.rem(step, 2) == 1, half, -half), RING)
-
     def cells_left(place, step):
-        target = far_first(step)
+        target = ring_target(step)
         sent = back_out.at[place, target]
         pltpu.make_async_copy(sent, sent, send_three.at[place, target]).wait()
 
@@ -400,7 +421,7 @@
 
         @pl.loop(1, RING + 1)
         def _(step):
-            target = far_first(step)
+            target = ring_target(step)
             within = lax.rem(13 * (target + RING - 8 * core) + RING * 12 - chunk * 12, RING)
             unit = chunk * 12 + within
             place = lax.div(unit, RING)
@@ -431,6 +452,9 @@
             lines_left(1)
             post_lines(2)
 
+    slope_y = spline_slope(offset_y)
+    slope_x = spline_slope(offset_x)
+    fill_z(spline_slope, slope_z)
     high, low = halves(dot(table[...], slope_z[...]))
     for chunk in range(CHUNKS):
         for place, value in enumerate((high, low, high)):
@@ -469,7 +493,7 @@
 
         @pl.loop(1, RING)
         def _(step):
-            target = far_first(step)
+            target = ring_target(step)
 
             @pl.when((place == 0) & (step <= 12))
             def _():
@@ -519,17 +543,20 @@
             cell_out.at[chunk, :, :, row], cell_in.at[chunk, :, row], recv_four.at[chunk]
         ).start()
 
-        @pl.loop(1, ROWS)
+        @pl.loop(0, ROWS)
         def _(step):
-            target = lax.rem(row + step, ROWS)
-            pltpu.make_async_remote_copy(
-                cell_out.at[chunk, :, :, target],
-                cell_in.at[chunk, :, row],
-                send_four.at[chunk],
-                recv_four.at[chunk],
-                device_id=in_rows(target),
-                device_id_type=MESH,
-            ).start()
+            target = row_target(step)
+
+            @pl.when(step != ROWS - 2)
+            def _():
+                pltpu.make_async_remote_copy(
+                    cell_out.at[chunk, :, :, target],
+                    cell_in.at[chunk, :, row],
+                    send_four.at[chunk],
+                    recv_four.at[chunk],
+                    device_id=in_rows(target),
+                    device_id_type=MESH,
+                ).start()
 
     cell_got = cell_in.reshape(CHUNKS, GROUPS, 128, 128)
     gathered[...] = jnp.zeros((MAIN + EDGE, 2 * SLOTS), F32)
@@ -638,7 +665,6 @@
                 pltpu.VMEM((MAIN, 3 * SLOTS), BF16),
                 pltpu.VMEM((3, MAIN, 128), F32),
                 pltpu.VMEM((MAIN, 3 * N), BF16),
-                pltpu.VMEM((N, 3 * SLOTS), BF16),
                 pltpu.VMEM((CHUNKS, 3 * 128, 2 * SLOTS), BF16),
                 pltpu.VMEM((4 * CX, EY * ROWS), F32),
                 pltpu.VMEM((128, 128), F32),

time: 83.4 us -> 81.8 us (0.981)
  Pallas kernels: 81.3 us -> 79.7 us
    pallas_call x1, Pallas kernels: 81.3 us -> 79.7 us  [per_device(): pl.pallas_call(kernel, out_shape=jax.ShapeDtypeStruct((3, 1, 1, SLOTS), F...]
where the time goes in v4:
time: 81.8 us; the launch traced here: 81.6 us
  Pallas kernels  79.7 us (97%)
  local copies, waits for them, and re-layouts  1.26 us (2%)
    pallas_call x1, Pallas kernels, per_device(): pl.pallas_call(kernel, out_shape=jax.ShapeDtypeStruct((3, 1, 1, SLOTS), F...  79.7 us

profile of v4, /device:TPU:1, one launch (start us, length us, event | category | flops | bytes accessed | tf_op | source)
XLA Modules:
  0.0 81.6 jit_solution(28791816125362984)
XLA Ops:
  0.7 79.7 %ewald.1 = f32[3,1,1,256]{3,2,1,0:T(1,128)} custom-call(f32[1,1,256]{2,1,0:T(1,128)} %atom_x_hbm.1, f32[1,1,256]{2,1,0:T(1,128)} %atom_y_hbm.1, f32[1,1,256]{2,1,0:T(1,128)} %atom_z_hbm.1, f32[1,1,256]{2,1,0:T(1,128)} %charges_hbm.1, s32[1,1]{1,0:T(1,128)S(6)} %copy.13.counts, f32[12,24,384]{2,1,0:T(8,128)} %background_hbm.1, ...), custom_call_target="tpu_custom_call" | custom-call | tf_op jit(solution)/shard_map/ewald/pallas_call | solution.py:654
  80.4 1.3 %copy.14 = f32[3,1,1,256]{3,2,1,0:T(1,128)} copy(f32[3,1,1,256]{3,2,1,0:T(1,128)} %ewald.1) | data formatting | bytes 6144

commit v5 on v4

--- a/solution.py
+++ b/solution.py
@@ -193,38 +193,6 @@
     def in_rows(index):
         return (ring, lax.div(index, 4), lax.rem(index, 4))
 
-    barrier = pltpu.get_barrier_semaphore()
-
-    def far_first(step, size):
-        half = lax.div(step, 2)
-        return size // 2 + jnp.where(lax.rem(step, 2) == 1, half, -half)
-
-    def ring_target(step):
-        return lax.rem(ring + far_first(step, RING), RING)
-
-    chip_x = 2 * lax.div(minor, 2) + lax.div(major, 4)
-    chip_y = lax.rem(major, 4)
-
-    def row_target(step):
-        x = lax.rem(chip_x + far_first(lax.div(step, 8) + 1, 4), 4)
-        y = lax.rem(chip_y + far_first(lax.rem(lax.div(step, 2), 4) + 1, 4), 4)
-        other = lax.rem(core + step, 2)
-        return (4 * lax.rem(x, 2) + y) * 4 + 2 * lax.div(x, 2) + other
-
-    @pl.loop(1, RING)
-    def _(step):
-        pl.semaphore_signal(
-            barrier, inc=1, device_id=in_ring(ring_target(step)), device_id_type=MESH
-        )
-
-    @pl.loop(0, ROWS)
-    def _(step):
-        @pl.when(step != ROWS - 2)
-        def _():
-            pl.semaphore_signal(
-                barrier, inc=1, device_id=in_rows(row_target(step)), device_id_type=MESH
-            )
-
     tables = [
         pltpu.make_async_copy(source, target, table_sem.at[place])
         for place, (source, target) in enumerate(
@@ -242,7 +210,42 @@
             )
         )
     ]
-    for copy in tables:
+    for copy in tables[:5]:
+        copy.start()
+
+    barrier = pltpu.get_barrier_semaphore()
+
+    def far_first(step, size):
+        half = lax.div(step, 2)
+        return size // 2 + jnp.where(lax.rem(step, 2) == 1, half, -half)
+
+    def ring_target(step):
+        return lax.rem(ring + far_first(step, RING), RING)
+
+    chip_x = 2 * lax.div(minor, 2) + lax.div(major, 4)
+    chip_y = lax.rem(major, 4)
+
+    def row_target(step):
+        x = lax.rem(chip_x + far_first(lax.div(step, 8) + 1, 4), 4)
+        y = lax.rem(chip_y + far_first(lax.rem(lax.div(step, 2), 4) + 1, 4), 4)
+        other = lax.rem(core + step, 2)
+        return (4 * lax.rem(x, 2) + y) * 4 + 2 * lax.div(x, 2) + other
+
+    @pl.loop(1, RING)
+    def _(step):
+        pl.semaphore_signal(
+            barrier, inc=1, device_id=in_ring(ring_target(step)), device_id_type=MESH
+        )
+
+    @pl.loop(0, ROWS)
+    def _(step):
+        @pl.when(step != ROWS - 2)
+        def _():
+            pl.semaphore_signal(
+                barrier, inc=1, device_id=in_rows(row_target(step)), device_id_type=MESH
+            )
+
+    for copy in tables[5:]:
         copy.start()
 
     for copy in tables[:4]:
@@ -278,13 +281,13 @@
             height_x[CX + place : CX + place + 1] * charged_y
         )
     high, low = halves(mixed[MAIN:, :])
+    edges = (
+        dot_nt(high, weight_z[:N, :])
+        + dot_nt(high, weight_z[2 * N :, :])
+        + dot_nt(low, weight_z[:N, :])
+    )
     for side in range(2):
-        rows = slice(side * 32, side * 32 + 32)
-        halo_out[side] = (
-            dot_nt(high[rows], weight_z[:N, :])
-            + dot_nt(high[rows], weight_z[2 * N :, :])
-            + dot_nt(low[rows], weight_z[:N, :])
-        )
+        halo_out[side] = edges[side * 32 : side * 32 + 32]
 
     pl.semaphore_wait(barrier, ROWS - 1 + RING - 1)
     sides = (lax.rem(ring + 1, RING), lax.rem(ring + RING - 1, RING))
@@ -558,15 +561,22 @@
                     device_id_type=MESH,
                 ).start()
 
+    lines_left(2)
+    for side in range(2):
+        pltpu.make_async_copy(halo_out.at[side], halo_out.at[side], send_halo.at[side]).wait()
+
+    @pl.loop(1, RING)
+    def _(step):
+        cells_left(n_places - 1, step)
+
     cell_got = cell_in.reshape(CHUNKS, GROUPS, 128, 128)
     gathered[...] = jnp.zeros((MAIN + EDGE, 2 * SLOTS), F32)
 
     @pl.loop(0, CHUNKS)
     def _(chunk):
         pltpu.make_async_copy(cell_in.at[chunk], cell_in.at[chunk], recv_four.at[chunk]).wait()
-        for group in range(GROUPS):
+        for side, group, first in ((0, 2, 2 * 128 + 6), (1, 0, 0)):
             cells[group * 128 : group * 128 + 128, :] = cell_got[chunk, group].T
-        for side, first in ((0, 2 * 128 + 6), (1, 0)):
             for place in range(2):
                 flank_out[chunk, side, place * EY : place * EY + EY, :] = cells[
                     pl.ds(first + place, EY, 8), :
@@ -579,6 +589,7 @@
                 device_id=in_ring(sides[side]),
                 device_id_type=MESH,
             ).start()
+        cells[128:256, :] = cell_got[chunk, 1].T
         high, low = halves(cells[...])
         gathered[:MAIN, :] += dot(jnp.concatenate([high, high, low], axis=1), pull_parts[chunk])
 
@@ -627,10 +638,6 @@
     for place, force in enumerate((force_x, force_y, force_z)):
         out[place, 0] = -live * jnp.sum(force, axis=0, keepdims=True)
 
-    lines_left(2)
-    for side in range(2):
-        pltpu.make_async_copy(halo_out.at[side], halo_out.at[side], send_halo.at[side]).wait()
-
     @pl.loop(0, CHUNKS)
     def _(chunk):
         sizes = cell_in.at[chunk, :, 0 : ROWS - 1]
@@ -638,10 +645,6 @@
         for side in range(2):
             sizes = flank_out.at[chunk, side]
             pltpu.make_async_copy(sizes, sizes, send_flank.at[chunk, side]).wait()
-
-    @pl.loop(1, RING)
-    def _(step):
-        cells_left(n_places - 1, step)
 
 
 def solution(mesh):

time: 81.8 us -> 81.9 us (level)
  no operation moved by 1% of the time
where the time goes in v5:
time: 81.9 us; the launch traced here: 81.8 us
  Pallas kernels  79.9 us (98%)
  local copies, waits for them, and re-layouts  1.26 us (2%)
    pallas_call x1, Pallas kernels, per_device(): pl.pallas_call(kernel, out_shape=jax.ShapeDtypeStruct((3, 1, 1, SLOTS), F...  79.9 us

profile of v5, /device:TPU:1, one launch (start us, length us, event | category | flops | bytes accessed | tf_op | source)
XLA Modules:
  0.0 81.8 jit_solution(18081240911128440546)
XLA Ops:
  0.7 79.9 %ewald.1 = f32[3,1,1,256]{3,2,1,0:T(1,128)} custom-call(f32[1,1,256]{2,1,0:T(1,128)} %atom_x_hbm.1, f32[1,1,256]{2,1,0:T(1,128)} %atom_y_hbm.1, f32[1,1,256]{2,1,0:T(1,128)} %atom_z_hbm.1, f32[1,1,256]{2,1,0:T(1,128)} %charges_hbm.1, s32[1,1]{1,0:T(1,128)S(6)} %copy.13.counts, f32[12,24,384]{2,1,0:T(8,128)} %background_hbm.1, ...), custom_call_target="tpu_custom_call" | custom-call | tf_op jit(solution)/shard_map/ewald/pallas_call | solution.py:657
  80.5 1.3 %copy.14 = f32[3,1,1,256]{3,2,1,0:T(1,128)} copy(f32[3,1,1,256]{3,2,1,0:T(1,128)} %ewald.1) | data formatting | bytes 6144

commit v6 on v5

--- a/solution.py
+++ b/solution.py
@@ -231,16 +231,12 @@
         other = lax.rem(core + step, 2)
         return (4 * lax.rem(x, 2) + y) * 4 + 2 * lax.div(x, 2) + other
 
-    @pl.loop(1, RING)
-    def _(step):
+    for step in range(1, RING):
         pl.semaphore_signal(
             barrier, inc=1, device_id=in_ring(ring_target(step)), device_id_type=MESH
         )
-
-    @pl.loop(0, ROWS)
-    def _(step):
-        @pl.when(step != ROWS - 2)
-        def _():
+    for step in range(ROWS):
+        if step != ROWS - 2:
             pl.semaphore_signal(
                 barrier, inc=1, device_id=in_rows(row_target(step)), device_id_type=MESH
             )
@@ -422,7 +418,7 @@
                     k * CX : k * CX + CX, tile * 128 : tile * 128 + 128
                 ]
 
-        @pl.loop(1, RING + 1)
+        @pl.loop(1, RING + 1, unroll=4)
         def _(step):
             target = ring_target(step)
             within = lax.rem(13 * (target + RING - 8 * core) + RING * 12 - chunk * 12, RING)
@@ -494,7 +490,7 @@
             back_out.at[place, ring], back_in.at[unit], recv_three.at[group]
         ).start()
 
-        @pl.loop(1, RING)
+        @pl.loop(1, RING, unroll=5)
         def _(step):
             target = ring_target(step)
 

time: 81.9 us -> 81.8 us (level)
  no operation moved by 1% of the time
where the time goes in v6:
time: 81.8 us; the launch traced here: 81.7 us
  Pallas kernels  79.8 us (98%)
  local copies, waits for them, and re-layouts  1.26 us (2%)
    pallas_call x1, Pallas kernels, per_device(): pl.pallas_call(kernel, out_shape=jax.ShapeDtypeStruct((3, 1, 1, SLOTS), F...  79.8 us

profile of v6, /device:TPU:1, one launch (start us, length us, event | category | flops | bytes accessed | tf_op | source)
XLA Modules:
  0.0 81.7 jit_solution(2854901573789146534)
XLA Ops:
  0.7 79.8 %ewald.1 = f32[3,1,1,256]{3,2,1,0:T(1,128)} custom-call(f32[1,1,256]{2,1,0:T(1,128)} %atom_x_hbm.1, f32[1,1,256]{2,1,0:T(1,128)} %atom_y_hbm.1, f32[1,1,256]{2,1,0:T(1,128)} %atom_z_hbm.1, f32[1,1,256]{2,1,0:T(1,128)} %charges_hbm.1, s32[1,1]{1,0:T(1,128)S(6)} %copy.13.counts, f32[12,24,384]{2,1,0:T(8,128)} %background_hbm.1, ...), custom_call_target="tpu_custom_call" | custom-call | tf_op jit(solution)/shard_map/ewald/pallas_call | solution.py:653
  80.4 1.3 %copy.14 = f32[3,1,1,256]{3,2,1,0:T(1,128)} copy(f32[3,1,1,256]{3,2,1,0:T(1,128)} %ewald.1) | data formatting | bytes 6144
